TPU v7x, 256 devices: a whole 4x4x8 slice. The times are simulated.
256 devices in a mesh: space: 32 (over x, z_hi, core), batch: 8 (over z_lo, y).
Axes of the slice: x: 4, y: 4, z: 8 (z_hi: 4, z_lo: 2; z = z_hi * 2 + z_lo), core: 2. Of those that a mesh axis runs over, the one named last changes fastest.
Arguments:
- inputs: bfloat16 [8, 64, 64, 64, 128], P('batch', 'space'), may hold values from -6 to 6
- cotangent: bfloat16 [8, 64, 64, 64, 128], P('batch', 'space'), may hold values from -6 to 6
- dense_weights: bfloat16 [32, 16, 16, 64, 128], P('space', 'batch'), may hold values from -0.5 to 0.5
- owner_table: int32 [16], replicated, may hold values from 0 to 15, each once
- hot_mask: int32 [32, 16, 16], P('space'), may hold values 0 or 1
- skip_weight: bfloat16 [64, 64], replicated, may hold values from -0.75 to 0.75
- bias_vector: float32 [64], replicated, may hold values from -3 to 3
- input_factor: bfloat16 [64, 16], replicated, may hold values from -0.75 to 0.75
- output_factor: bfloat16 [64, 16], replicated, may hold values from -1.5 to 1.5
- first_factor: float32 [2, 32, 16], replicated, may hold values from -4 to 4
- second_factor: float32 [32, 16], replicated, may hold values from -5 to 5
- third_factor: float32 [16, 16], replicated, may hold values from -5 to 5
Outputs:
- output: bfloat16 [8, 64, 64, 64, 128], P('batch', 'space')
- input_grad: bfloat16 [8, 64, 64, 64, 128], P('batch', 'space')
- dense_grad: float32 [32, 16, 16, 64, 128], P('space', 'batch')
- input_factor_grad: float32 [64, 16], replicated
- output_factor_grad: float32 [64, 16], replicated
- first_factor_grad: float32 [2, 32, 16], replicated
- second_factor_grad: float32 [32, 16], replicated
- third_factor_grad: float32 [16, 16], replicated
- skip_grad: float32 [64, 64], replicated
- bias_grad: float32 [64], replicated
Inputs may be any that keep to these rules, and one draw needn't show every extreme that they name: `owner_table`: each of 0 to 15 appears once.
All inputs are finite; a program needn't handle non-finite values. No bound on the sum of `hot_mask` on one device may be relied on, other than what follows from the above.
Results may differ from a plain program's by a relative error of at most 0.025.
Values may be sent and summed in bfloat16 or wider, within the bound.
A program may use at most 128 MiB of HBM per device.

v0:
```python
import math

import jax
import jax.numpy as jnp
import ml_dtypes
import numpy as np
from jax import lax
from jax.experimental import pallas as pl
from jax.experimental.pallas import tpu as pltpu
from jax.sharding import PartitionSpec as P

MESH = pl.DeviceIdType.MESH
F32 = jnp.float32
BF16 = jnp.bfloat16
HIGH = lax.Precision.HIGHEST

C = 64
N1 = 64
N2 = 64
N3 = 128
K1 = 32
K2 = 32
K3 = 16
L2 = 16
R = 16
SAMPLES = 8
NS = 32
NB = 8
ROWS = N2 // NS
CG = 8
CQ = 8
SLOTS = L2 // NB
GRAD_SCALE = float(SAMPLES * N1 * N2 * N3) ** (-0.5)


def rounded(values):
    return np.asarray(values, np.float32).astype(ml_dtypes.bfloat16)


def twiddles(frequency, length):
    index = np.mod(frequency[:, None] * np.arange(length)[None, :], length)
    radians = index.astype(np.float32) * np.float32(2.0 * math.pi / length)
    return np.cos(radians), np.sin(radians)


def retained(amount):
    position = np.arange(amount)
    return np.where(position % 2 == 0, position // 2, -((position + 1) // 2))


def build_tables():
    factor = float(N1 * N2 * N3 * K1 * K2 * K3) ** (-0.25)
    cos1, sin1 = twiddles(retained(K1), N1)
    t0 = np.float32(factor) * cos1
    t1 = np.float32(-factor) * sin1
    one = np.block([[t0, -t1], [t1, t0]])
    cos2, sin2 = twiddles(retained(K2), N2)
    two = np.zeros((2, K2, N2, 2), np.float32)
    two[0, :, :, 0] = cos2
    two[0, :, :, 1] = sin2
    two[1, :, :, 0] = -sin2
    two[1, :, :, 1] = cos2
    two = two.reshape(2 * K2, 2 * N2)
    cos3, sin3 = twiddles(np.arange(K3), N3)
    three = np.zeros((CQ, N3, 2, K3, CQ), np.float32)
    for q in range(CQ):
        three[q, :, 0, :, q] = cos3.T
        three[q, :, 1, :, q] = -sin3.T
    three = three.reshape(CQ * N3, 2 * K3 * CQ)
    eye = np.eye(R, dtype=np.float32)

    def tiled(signs):
        return np.concatenate([sign * eye for sign in signs] + [np.zeros((R, 64), np.float32)], axis=1)

    patterns = np.concatenate(
        [
            tiled((1, 0, 0, 1)),
            tiled((1, 0, 1, 0)),
            tiled((0, 1, -1, 0)),
            tiled((0, 1, 0, 1)),
            tiled((1, 0, 0, -1)),
            tiled((0, 1, 1, 0)),
        ],
        axis=1,
    )
    spread = np.stack([tiled((1, 1, 1, 1)), tiled((1, 1, 0, 0)), tiled((0, 0, 1, 1))])
    select = np.zeros((K3, K3, 128), np.float32)
    for k in range(K3):
        select[k, k] = 1.0
    return (
        rounded(three),
        rounded(three.T),
        rounded(one),
        rounded(one.T),
        rounded(two),
        rounded(two.T),
        rounded(patterns),
        spread.astype(np.float32),
        rounded(select.reshape(K3, K3 * 128)),
    )


def dot(a, b, precision=None):
    return jnp.dot(a, b, preferred_element_type=F32, precision=precision)


def dot_nt(a, b, precision=None):
    return lax.dot_general(
        a, b, (((1,), (1,)), ((), ())), preferred_element_type=F32, precision=precision
    )


def dot_tn(a, b):
    return lax.dot_general(a, b, (((0,), (0,)), ((), ())), preferred_element_type=F32)


def lanes(shape):
    return lax.broadcasted_iota(jnp.int32, shape, len(shape) - 1)


def rows(shape):
    return lax.broadcasted_iota(jnp.int32, shape, 0)


def swap_groups(parts):
    parts = list(parts)
    group = lanes(parts[0].shape) // CQ
    for bit in (1, 2, 4, 8):
        low = (group & bit) == 0
        for a in range(16):
            if a & bit:
                continue
            first, second = parts[a], parts[a + bit]
            parts[a] = jnp.where(low, first, pltpu.roll(second, 8 * bit, 1))
            parts[a + bit] = jnp.where(low, pltpu.roll(first, 128 - 8 * bit, 1), second)
    return parts


def left_by(value, amount):
    return pltpu.roll(value, 128 - amount, 1)


def drain(block, sem):
    pltpu.make_async_copy(block, block, sem).wait()


def backward_rows(blocks, zf, left_v, one_t):
    zf[...] = blocks.reshape(NS * 32, 128).astype(F32)
    for n in range(ROWS):
        block = jnp.concatenate(
            [
                jnp.concatenate(
                    [
                        zf[pl.ds(n * 16 + part * 8 + g, K1, stride=32), :].astype(BF16)
                        for part in range(2)
                    ],
                    axis=0,
                )
                for g in range(CG)
            ],
            axis=1,
        )
        field = dot(one_t, block).astype(BF16)
        for g in range(CG):
            left_v[n, g * N1 : (g + 1) * N1, :128] = field[:N1, g * 128 : (g + 1) * 128]
            left_v[n, g * N1 : (g + 1) * N1, 128:] = field[N1:, g * 128 : (g + 1) * 128]


def each_pair(n, left_v, three_t, body):
    @pl.loop(0, CQ // 2)
    def _(pair):
        column = pl.multiple_of(pair * 256, 256)
        field = dot(left_v[n], three_t[:, pl.ds(column, 256)])
        for half in range(2):
            body(pair * 2 + half, field[:, half * 128 : (half + 1) * 128].reshape(CG, N1, N3))


def kernel(
    owner_ref,
    bias_ref,
    x_hbm,
    three_hbm,
    one_hbm,
    hot_hbm,
    skip_hbm,
    fin_hbm,
    fout_hbm,
    first_hbm,
    second_hbm,
    third_hbm,
    two_hbm,
    two_t_hbm,
    pat_hbm,
    spread_hbm,
    select_hbm,
    one_t_hbm,
    three_t_hbm,
    cot_hbm,
    w_hbm,
    out_hbm,
    skip_out_hbm,
    dg_hbm,
    blocks_ref,
    red_ref,
    x_ref,
    three_ref,
    one_ref,
    hot_ref,
    skip_ref,
    fin_ref,
    fout_ref,
    first_ref,
    second_ref,
    third_ref,
    two_ref,
    two_t_ref,
    pat_ref,
    spread_ref,
    select_ref,
    one_t_ref,
    three_t_ref,
    cot_v,
    w_v,
    out_v,
    gp_v,
    dg_v,
    skip_v,
    kron_v,
    left_v,
    zf,
    sbuf,
    rbuf,
    bsend,
    brecv,
    sm,
    s16,
    maskf,
    ph,
    coef_b,
    prod_v,
    fac_v,
    xs,
    bz,
    sgs,
    pk,
    r_batch,
    r_near,
    r_far,
    r_all,
    part_near,
    part_far,
    part_all,
    in_sem,
    out_sem,
    ssend,
    srecv,
    bssem,
    brsem,
    rsend,
    rrecv,
):
    me_s = lax.axis_index("space")
    me_b = lax.axis_index("batch")
    def fetch(src, dst, index):
        copy = pltpu.make_async_copy(src, dst, in_sem.at[index])
        copy.start()
        return copy

    x_copies = [fetch(x_hbm.at[n], x_ref.at[n], n) for n in range(ROWS)]
    three_copy = fetch(three_hbm, three_ref, 2)
    one_copy = fetch(one_hbm, one_ref, 3)
    small_copies = [
        fetch(src, dst, 4 + index)
        for index, (src, dst) in enumerate(
            (
                (hot_hbm, hot_ref),
                (skip_hbm, skip_ref),
                (fin_hbm, fin_ref),
                (fout_hbm, fout_ref),
                (first_hbm, first_ref),
                (second_hbm, second_ref),
                (third_hbm, third_ref),
                (two_hbm, two_ref),
                (two_t_hbm, two_t_ref),
                (pat_hbm, pat_ref),
                (spread_hbm, spread_ref),
                (select_hbm, select_ref),
                (one_t_hbm, one_t_ref),
                (three_t_hbm, three_t_ref),
            )
        )
    ]
    cot_copy = fetch(cot_hbm, cot_v, 18)
    w_copy = fetch(w_hbm.at[0], w_v, 19)

    barrier = pltpu.get_barrier_semaphore()

    @pl.loop(1, NS)
    def _(d):
        pl.semaphore_signal(
            barrier, inc=1, device_id={"space": lax.rem(me_s + d, NS)}, device_id_type=MESH
        )

    @pl.loop(1, NB)
    def _(d):
        pl.semaphore_signal(
            barrier, inc=1, device_id={"batch": lax.rem(me_b + d, NB)}, device_id_type=MESH
        )

    def space_start(phase):
        @pl.loop(1, NS)
        def _(d):
            peer = lax.rem(me_s + d, NS)
            pltpu.make_async_remote_copy(
                src_ref=sbuf.at[phase, peer],
                dst_ref=rbuf.at[phase, me_s],
                send_sem=ssend.at[phase],
                recv_sem=srecv.at[phase],
                device_id={"space": peer},
                device_id_type=MESH,
            ).start()

        rbuf[phase, me_s] = sbuf[phase, me_s]

    def space_wait(phase):
        drain(rbuf.at[phase, pl.ds(0, NS - 1)], srecv.at[phase])

    def batch_start(phase):
        @pl.loop(1, NB)
        def _(d):
            peer = lax.rem(me_b + d, NB)
            pltpu.make_async_remote_copy(
                src_ref=bsend.at[phase, peer],
                dst_ref=brecv.at[phase, me_b],
                send_sem=bssem.at[phase],
                recv_sem=brsem.at[phase],
                device_id={"batch": peer},
                device_id_type=MESH,
            ).start()

        brecv[phase, me_b] = bsend[phase, me_b]

    def batch_wait(phase):
        drain(brecv.at[phase, pl.ds(0, NB - 1)], brsem.at[phase])

    def forward_cells(src, phase, copies):
        for n in range(ROWS):
            if copies is not None:
                copies[n].wait()
            total = None
            for q in range(0, CQ, 2):
                pair = jnp.concatenate(
                    [src[n, :, q].reshape(CG * N1, N3), src[n, :, q + 1].reshape(CG * N1, N3)], axis=1
                )
                term = dot(pair, three_ref[q * N3 : (q + 2) * N3, :])
                total = term if total is None else total + term
            total = total.astype(BF16)
            right = jnp.concatenate(
                [
                    jnp.concatenate(
                        [total[g * N1 : (g + 1) * N1, :128], total[g * N1 : (g + 1) * N1, 128:]], axis=0
                    )
                    for g in range(CG)
                ],
                axis=1,
            )
            modes = dot(one_ref[...], right)
            for g in range(CG):
                for part in range(2):
                    zf[pl.ds(n * 16 + part * 8 + g, K1, stride=32), :] = modes[
                        part * K1 : (part + 1) * K1, g * 128 : (g + 1) * 128
                    ]
        sbuf[phase] = zf[...].astype(BF16).reshape(NS, 32, 128)

    def modes_in(phase, table):
        zf[...] = rbuf[phase].reshape(NS * 32, 128).astype(F32)
        cells = jnp.concatenate(
            [zf[pl.ds(g, 2 * N2, stride=8), :].astype(BF16) for g in range(CG)], axis=1
        )
        modes = dot(table, cells)
        parts = [
            modes[part * K2 : (part + 1) * K2, g * 128 : (g + 1) * 128]
            for part in range(2)
            for g in range(CG)
        ]
        return swap_groups(parts)

    def modes_out(by_frequency, table, phase):
        parts = swap_groups(by_frequency)
        spectrum = jnp.concatenate(
            [
                jnp.concatenate([parts[part * CG + g] for g in range(CG)], axis=1).astype(BF16)
                for part in range(2)
            ],
            axis=0,
        )
        cells = dot(table, spectrum)
        for g in range(CG):
            zf[pl.ds(g, 2 * N2, stride=8), :] = cells[:, g * 128 : (g + 1) * 128]
        sbuf[phase] = zf[...].astype(BF16).reshape(NS, 32, 128)

    def mix_channels(src, with_bias):
        @pl.loop(0, N1 // 16)
        def _(step):
            cut = pl.ds(pl.multiple_of(step * 16, 16), 16)
            right = jnp.concatenate(
                [src[n, :, :, cut, :].reshape(C * 16, N3) for n in range(ROWS)], axis=1
            )
            mixed = dot(kron_v[...], right)
            for n in range(ROWS):
                value = mixed[:, n * N3 : (n + 1) * N3].reshape(C, 16, N3)
                if with_bias:
                    value = jnp.concatenate([value[c : c + 1] + bias_ref[c] for c in range(C)], axis=0)
                skip_v[n, :, :, cut, :] = value.astype(BF16).reshape(CG, CQ, 16, N3)

    spread_rows = (rows((C * 16, C)) // 16 == lanes((C * 16, C))).astype(F32)
    spread_half = spread_rows.astype(BF16)

    def build_kron(base):
        expanded = dot(spread_half, base).astype(BF16)
        for block in range(4):
            cut = slice(block * 256, (block + 1) * 256)
            full = dot_nt(expanded[cut], spread_half)
            same = (rows((256, 1024)) & 15) == (lanes((256, 1024)) & 15)
            kron_v[cut, :] = jnp.where(same, full, 0.0).astype(BF16)

    three_copy.wait()
    one_copy.wait()
    forward_cells(x_ref, 0, x_copies)
    pl.semaphore_wait(barrier, NS - 1 + NB - 1)
    space_start(0)

    for copy in small_copies:
        copy.wait()
    side = (2 * K2, 2 * K2)

    def permutation(index, other):
        position = index & (K2 - 1)
        target = index
        for slot in range(L2):
            target = jnp.where(position == slot, index - position + owner_ref[slot], target)
        return (target == other).astype(F32)

    perm = permutation(rows(side), lanes(side))
    perm_t = permutation(lanes(side), rows(side))
    perm_half = perm.astype(BF16)
    two = dot(perm_half, two_ref[...]).astype(BF16)
    two_t = dot_nt(two_t_ref[...], perm_half).astype(BF16)
    second = dot_nt(perm[:K2, :K2], second_ref[...], HIGH)
    second_l = dot(second, spread_ref[0], HIGH)
    third_l = dot(third_ref[...], spread_ref[0], HIGH)
    own = (lanes((8, K1)) == me_s).astype(F32)
    first_l = (
        dot(dot_nt(own, first_ref[0], HIGH), spread_ref[1], HIGH)
        + dot(dot_nt(own, first_ref[1], HIGH), spread_ref[2], HIGH)
    )[0:1]
    for k in range(K3):
        ph[k * K2 : (k + 1) * K2, :] = first_l * (second_l * third_l[k : k + 1])
    hot = dot(perm_half[:L2, :L2], hot_ref[0].astype(F32).astype(BF16)).astype(BF16)
    spread_hot = dot(hot, select_ref[...])
    for k in range(K3):
        maskf[k] = spread_hot[:, k * 128 : (k + 1) * 128]

    def expand(factor, top, bottom, width):
        pieces = [
            dot_tn(factor, pat_ref[:, start * 128 : start * 128 + width]) for start in (top, bottom)
        ]
        return jnp.concatenate(pieces, axis=0).astype(BF16)

    fin_all = expand(fin_ref[...], 0, 2, 256)
    fin_b = fin_all[:, 128:]
    fout_b = expand(fout_ref[...], 1, 3, 128)
    fout_c = expand(fout_ref[...], 4, 5, 128)

    build_kron(skip_ref[...].astype(F32).T.astype(BF16))
    mix_channels(x_ref, True)

    space_wait(0)
    spectrum = modes_in(0, two)
    for k in range(K3):
        sm[k * K2 : (k + 1) * K2, :] = spectrum[k]

    def slots_out(phase):
        for owner in range(NB):
            for slot in range(SLOTS):
                bsend[phase, owner, slot * K3 : (slot + 1) * K3, :] = sm[
                    pl.ds(owner * SLOTS + slot, K3, stride=K2), :
                ].astype(BF16)

    def slots_in(phase):
        bz[...] = brecv[phase].reshape(NB * 32, 128).astype(F32)
        for slot in range(L2):
            sm[pl.ds(slot, K3, stride=K2), :] = bz[slot * K3 : (slot + 1) * K3, :]

    slots_out(0)
    batch_start(0)
    s16[...] = sm[...].astype(BF16)
    coef = dot(s16[...], fin_all)
    coef_b[...] = coef[:, 128:]
    prod_v[...] = (coef[:, :128] * ph[...]).astype(BF16)
    fac_v[...] = dot_nt(prod_v[...], fout_b)
    w_copy.wait()
    batch_wait(0)
    xs[...] = brecv[0].reshape(NB * 32, 128).astype(F32)
    sign = jnp.where(lanes((8, 128)) < 64, -1.0, 1.0)
    for index in range(SLOTS * K3):
        slot, k = divmod(index, K3)
        value = xs[pl.ds(index, NB, stride=32), :]
        left = jnp.concatenate([value, pltpu.roll(value, 64, 1)], axis=0)[:, :C].astype(BF16)
        both = dot(left, w_v[slot, k])
        bz[pl.ds(index, NB, stride=32), :] = both[:8] + sign * pltpu.roll(both[8:], 64, 1)
    bsend[1] = bz[...].astype(BF16).reshape(NB, 32, 128)
    batch_start(1)
    batch_wait(1)
    slots_in(1)
    out_spec = []
    for k in range(K3):
        low = jnp.where(
            maskf[k] > 0.0, sm[k * K2 : k * K2 + L2, :], fac_v[k * K2 : k * K2 + L2, :]
        )
        out_spec.append(jnp.concatenate([low, fac_v[k * K2 + L2 : (k + 1) * K2, :]], axis=0))
    modes_out(out_spec, two_t, 1)
    space_start(1)
    cot_copy.wait()
    space_wait(1)
    backward_rows(rbuf[1], zf, left_v, one_t_ref[...])

    for n in range(ROWS):

        def activate(q, field):
            v = field + skip_v[n, :, q].astype(F32)
            square = v * v
            k0 = math.sqrt(2.0 / math.pi)
            gate = 0.5 * jnp.tanh(v * (k0 + (k0 * 0.044715) * square)) + 0.5
            active = v * gate
            out_v[n, :, q] = active.astype(BF16)
            slope = gate + active * (1.0 - gate) * (2.0 * k0 + (6.0 * k0 * 0.044715) * square)
            gp_v[n, :, q] = (cot_v[n, :, q].astype(F32) * slope).astype(BF16)

        each_pair(n, left_v, three_t_ref, activate)
    out_copy = pltpu.make_async_copy(out_v, out_hbm, out_sem.at[0])
    out_copy.start()

    forward_cells(gp_v, 2, None)
    space_start(2)

    build_kron(skip_ref[...])
    mix_channels(gp_v, False)
    skip_copy = pltpu.make_async_copy(skip_v, skip_out_hbm, out_sem.at[2])
    skip_copy.start()
    same = ((rows((16, 256)) & 15) == (lanes((16, 256)) & 15)).astype(F32)
    ones = jnp.ones((16, ROWS * 4 * N3), BF16)

    def cut_channels(src, start):
        return jnp.concatenate(
            [
                src[n, pl.ds(start * 2, 2), :, b * 16 : (b + 1) * 16, :].reshape(256, N3)
                for n in range(ROWS)
                for b in range(N1 // 16)
            ],
            axis=1,
        )

    for column in range(4):
        grads = cut_channels(gp_v, column)
        here = slice(column * 256, (column + 1) * 256)
        sgs[C : C + 16, here] = dot_nt(ones, grads)

        @pl.loop(0, 4)
        def _(block):
            full = dot_nt(cut_channels(x_ref, block), grads).reshape(16, 16, 256)
            sgs[pl.ds(pl.multiple_of(block * 16, 16), 16), here] = jnp.sum(full * same[None], axis=1)

    skip_grad = dot(sgs[...], spread_rows, HIGH)

    space_wait(2)
    grad_spec = modes_in(2, two)
    cold = []
    for k in range(K3):
        low = grad_spec[k][:L2]
        sm[k * K2 : k * K2 + L2, :] = low * maskf[k]
        cold.append(
            jnp.concatenate([low * (1.0 - maskf[k]), grad_spec[k][L2:]], axis=0).astype(BF16)
        )
    slots_out(2)
    batch_start(2)
    cold = jnp.concatenate(cold, axis=0)
    back = dot(cold, fout_c)
    prod_back = (back * ph[...]).astype(BF16)
    fac_v[...] = dot_nt(prod_back, fin_b)
    in_full = dot_tn(s16[...], prod_back)
    out_full = dot_tn(cold, prod_v[...])
    back = back * coef_b[...]
    first_sum = jnp.zeros((K2, 128), F32)
    second_sum = jnp.zeros((K2, 128), F32)
    third_rows = []
    for k in range(K3):
        term = back[k * K2 : (k + 1) * K2]
        by_third = term * third_l[k : k + 1]
        first_sum = first_sum + by_third * second_l
        second_sum = second_sum + by_third * first_l
        third_rows.append(jnp.sum(term * first_l * second_l, axis=0, keepdims=True))
    first_row = jnp.sum(first_sum, axis=0, keepdims=True)
    third_sum = jnp.concatenate(third_rows, axis=0)

    def folded(full):
        pairs = full + left_by(full, 32)
        return pairs[:C] + left_by(pairs[C:], 16)

    shape = (C, 128)
    lane, row = lanes(shape), rows(shape)

    def below(value):
        return jnp.concatenate([value, jnp.zeros((C - value.shape[0], 128), F32)], axis=0)

    def fold_all(value):
        pairs = value + left_by(value, 16)
        return pairs + left_by(pairs, 32)

    second_part = dot(perm_t[:K2, :K2], fold_all(second_sum), HIGH)
    third_part = fold_all(third_sum)
    first_part = first_row + left_by(first_row, 16)
    middle = jnp.concatenate([second_part, third_part, jnp.zeros((16, 128), F32)], axis=0)
    zero64 = jnp.zeros((C, 64), F32)
    wide = jnp.concatenate([skip_grad[:C], zero64], axis=1)
    bias_row = jnp.concatenate([skip_grad[C : C + 1], zero64[:1]], axis=1)
    packed = jnp.where(lane < 64, wide, 0.0)
    packed = jnp.where((lane >= 64) & (lane < 80), pltpu.roll(folded(in_full), 64, 1), packed)
    packed = jnp.where((lane >= 80) & (lane < 96), pltpu.roll(folded(out_full), 80, 1), packed)
    inside = (lane >= 96) & (lane < 112)
    packed = jnp.where(inside, pltpu.roll(middle, 96, 1), packed)
    for piece in range(4):
        moved = pltpu.roll(bias_row, 96 - 16 * piece, 1)
        packed = jnp.where(inside & (row == 48 + piece), moved, packed)
    last = lane >= 112
    packed = jnp.where(last & (row == me_s), pltpu.roll(first_part, 112, 1), packed)
    packed = jnp.where(last & (row == me_s + 32), pltpu.roll(first_part, 80, 1), packed)
    pk[...] = (packed * GRAD_SCALE).reshape(NB, 8, 128)

    def send(src, dst, step, to):
        pltpu.make_async_remote_copy(
            src_ref=src,
            dst_ref=dst,
            send_sem=rsend.at[step],
            recv_sem=rrecv.at[step],
            device_id=to,
            device_id_type=MESH,
        ).start()

    near = (me_s // 8) * 2 + lax.rem(me_s, 2)
    far = lax.rem(me_s // 2, 4)

    @pl.loop(1, NB)
    def _(d):
        peer = lax.rem(me_b + d, NB)
        send(pk.at[peer], r_batch.at[me_b], 0, {"batch": peer})

    r_batch[me_b] = pk[me_b]

    batch_wait(2)
    bz[...] = brecv[2].reshape(NB * 32, 128).astype(F32)
    for index in range(SLOTS * K3):
        slot, k = divmod(index, K3)
        value = xs[pl.ds(index, NB, stride=32), :]
        grad = bz[pl.ds(index, NB, stride=32), :]
        left = jnp.concatenate([value, pltpu.roll(value, 64, 1)], axis=0).astype(BF16)
        grads = jnp.concatenate([grad, -sign * pltpu.roll(grad, 64, 1)], axis=0).astype(BF16)
        weights = w_v[slot, k]
        both = dot_nt(grads, jnp.concatenate([weights, weights], axis=0))
        bz[pl.ds(index, NB, stride=32), :] = jnp.where(sign < 0.0, both[:8], both[8:])
        dg_v[slot, k] = dot_tn(left, grads)[:C]
    bsend[3] = bz[...].astype(BF16).reshape(NB, 32, 128)
    batch_start(3)
    dg_copy = pltpu.make_async_copy(dg_v, dg_hbm.at[0], out_sem.at[1])
    dg_copy.start()

    drain(r_batch.at[pl.ds(0, NB - 1)], rrecv.at[0])
    part_near[...] = jnp.sum(r_batch[...], axis=0)

    @pl.loop(1, 8)
    def _(d):
        slot = lax.rem(near + d, 8)
        peer = (slot // 2) * 8 + far * 2 + lax.rem(slot, 2)
        send(part_near, r_near.at[near], 1, {"space": peer})

    r_near[near] = part_near[...]

    batch_wait(3)
    slots_in(3)
    grad_spectrum = []
    for k in range(K3):
        low = fac_v[k * K2 : k * K2 + L2, :] + sm[k * K2 : k * K2 + L2, :]
        grad_spectrum.append(
            jnp.concatenate([low, fac_v[k * K2 + L2 : (k + 1) * K2, :]], axis=0)
        )
    modes_out(grad_spectrum, two_t, 3)
    space_start(3)


    drain(r_near.at[pl.ds(0, 7)], rrecv.at[1])
    part_far[...] = jnp.sum(r_near[...], axis=0)

    @pl.loop(1, 4)
    def _(d):
        slot = lax.rem(far + d, 4)
        peer = (near // 2) * 8 + slot * 2 + lax.rem(near, 2)
        send(part_far, r_far.at[far], 2, {"space": peer})

    r_far[far] = part_far[...]
    drain(r_far.at[pl.ds(0, 3)], rrecv.at[2])
    part_all[...] = jnp.sum(r_far[...], axis=0)

    @pl.loop(1, NB)
    def _(d):
        send(part_all, r_all.at[me_b], 3, {"batch": lax.rem(me_b + d, NB)})

    r_all[me_b] = part_all[...]
    drain(r_all.at[pl.ds(0, NB - 1)], rrecv.at[3])
    red_ref[...] = r_all[...].reshape(C, 128)

    space_wait(3)
    blocks_ref[...] = rbuf[3]
    for phase in range(4):
        drain(sbuf.at[phase, pl.ds(0, NS - 1)], ssend.at[phase])
        drain(bsend.at[phase, pl.ds(0, NB - 1)], bssem.at[phase])
    drain(pk.at[pl.ds(0, NB - 1)], rsend.at[0])
    drain(r_near.at[pl.ds(0, 7)], rsend.at[1])
    drain(r_far.at[pl.ds(0, 3)], rsend.at[2])
    drain(r_all.at[pl.ds(0, NB - 1)], rsend.at[3])
    out_copy.wait()
    dg_copy.wait()
    skip_copy.wait()


def finish_kernel(
    blocks_ref,
    packed_ref,
    one_t_ref,
    three_t_hbm,
    skip_hbm,
    out_in,
    dg_in,
    out_hbm,
    ig_hbm,
    dg_hbm,
    fin_hbm,
    fout_hbm,
    first_hbm,
    second_hbm,
    third_hbm,
    mix_hbm,
    bias_hbm,
    three_t_v,
    out_v,
    dg_v,
    skip_v,
    ig_v,
    left_v,
    zf,
    fin_v,
    fout_v,
    first_v,
    second_v,
    third_v,
    mix_v,
    bias_v,
    sem,
):
    def copy(src, dst, index):
        started = pltpu.make_async_copy(src, dst, sem.at[index])
        started.start()
        return started

    three_copy = copy(three_t_hbm, three_t_v, 2)
    skip_copies = [copy(skip_hbm.at[n], skip_v.at[n], n) for n in range(ROWS)]
    moved_in = [copy(out_in, out_v, 3), copy(dg_in, dg_v, 4)]
    backward_rows(blocks_ref[...], zf, left_v, one_t_ref[...])
    packed = packed_ref[...]
    turned = packed.T
    fin_v[...] = turned[64:80]
    fout_v[...] = turned[80:96]
    second_v[...] = turned[96:112, :K2]
    first_v[0] = turned[112:, :K1]
    first_v[1] = turned[112:, K1:]
    third_v[...] = left_by(packed, 96)[K2 : K2 + K3, :R]
    mix_v[...] = packed[:, :C]
    bias = jnp.zeros((1, 128), F32)
    lane = lanes((1, 128))
    for piece in range(4):
        moved = pltpu.roll(packed[48 + piece : 49 + piece], (32 + 16 * piece) % 128, 1)
        bias = jnp.where((lane >= 16 * piece) & (lane < 16 * (piece + 1)), moved, bias)
    bias_v[...] = bias[:, :C]
    small = (
        (fin_v, fin_hbm),
        (fout_v, fout_hbm),
        (first_v, first_hbm),
        (second_v, second_hbm),
        (third_v, third_hbm),
        (mix_v, mix_hbm),
        (bias_v, bias_hbm),
    )
    waits = [copy(src, dst, 5 + index) for index, (src, dst) in enumerate(small)]
    for arrived in moved_in:
        arrived.wait()
    waits += [copy(out_v, out_hbm, 14), copy(dg_v, dg_hbm, 15)]
    three_copy.wait()
    for n in range(ROWS):
        skip_copies[n].wait()

        def finish(q, field):
            ig_v[n, :, q] = (field + skip_v[n, :, q].astype(F32)).astype(BF16)

        each_pair(n, left_v, three_t_v, finish)
        waits.append(copy(ig_v.at[n], ig_hbm.at[n], 12 + n))
    for started in waits:
        started.wait()


def local(
    inputs,
    cotangent,
    dense_weights,
    owner_table,
    hot_mask,
    skip_weight,
    bias_vector,
    input_factor,
    output_factor,
    first_factor,
    second_factor,
    third_factor,
):
    field = (ROWS, CG, CQ, N1, N3)
    three, three_t, one, one_t, two, two_t, patterns, spread, select = [
        jnp.asarray(table) for table in build_tables()
    ]
    vmem = pl.BlockSpec(memory_space=pltpu.VMEM)
    smem = pl.BlockSpec(memory_space=pltpu.SMEM)
    hbm = pl.BlockSpec(memory_space=pltpu.HBM)
    dense = (SLOTS, K3, C, 2 * C)
    operands = (
        inputs.reshape(field),
        three,
        one,
        hot_mask,
        skip_weight,
        input_factor.T,
        output_factor.T,
        jnp.swapaxes(first_factor, 1, 2),
        second_factor.T,
        third_factor,
        two,
        two_t,
        patterns,
        spread,
        select,
        one_t,
        three_t,
        cotangent.reshape(field),
    )
    blocks = (NS, 32, 128)
    output, skip_part, dense_grad, received, packed = pl.pallas_call(
        kernel,
        out_shape=(
            jax.ShapeDtypeStruct(field, BF16),
            jax.ShapeDtypeStruct(field, BF16),
            jax.ShapeDtypeStruct((1,) + dense, F32),
            jax.ShapeDtypeStruct(blocks, BF16),
            jax.ShapeDtypeStruct((C, 128), F32),
        ),
        in_specs=[smem, smem] + [hbm] * 19,
        out_specs=(hbm, hbm, hbm, vmem, vmem),
        scratch_shapes=[pltpu.VMEM(value.shape, value.dtype) for value in operands]
        + [
            pltpu.VMEM(dense, BF16),
            pltpu.VMEM(field, BF16),
            pltpu.VMEM(field, BF16),
            pltpu.VMEM(dense, F32),
            pltpu.VMEM(field, BF16),
            pltpu.VMEM((C * 16, C * 16), BF16),
            pltpu.VMEM((ROWS, CG * N1, 256), BF16),
            pltpu.VMEM((NS * 32, 128), F32),
            pltpu.VMEM((4,) + blocks, BF16),
            pltpu.VMEM((4,) + blocks, BF16),
            pltpu.VMEM((4, NB, 32, 128), BF16),
            pltpu.VMEM((4, NB, 32, 128), BF16),
            pltpu.VMEM((K3 * K2, 128), F32),
            pltpu.VMEM((K3 * K2, 128), BF16),
            pltpu.VMEM((K3, L2, 128), F32),
            pltpu.VMEM((K3 * K2, 128), F32),
            pltpu.VMEM((K3 * K2, 128), F32),
            pltpu.VMEM((K3 * K2, 128), BF16),
            pltpu.VMEM((K3 * K2, 128), F32),
            pltpu.VMEM((NB * 32, 128), F32),
            pltpu.VMEM((NB * 32, 128), F32),
            pltpu.VMEM((C + 16, C * 16), F32),
            pltpu.VMEM((NB, 8, 128), F32),
            pltpu.VMEM((NB, 8, 128), F32),
            pltpu.VMEM((8, 8, 128), F32),
            pltpu.VMEM((4, 8, 128), F32),
            pltpu.VMEM((NB, 8, 128), F32),
            pltpu.VMEM((8, 128), F32),
            pltpu.VMEM((8, 128), F32),
            pltpu.VMEM((8, 128), F32),
            pltpu.SemaphoreType.DMA((20,)),
            pltpu.SemaphoreType.DMA((3,)),
            pltpu.SemaphoreType.DMA((4,)),
            pltpu.SemaphoreType.DMA((4,)),
            pltpu.SemaphoreType.DMA((4,)),
            pltpu.SemaphoreType.DMA((4,)),
            pltpu.SemaphoreType.DMA((4,)),
            pltpu.SemaphoreType.DMA((4,)),
        ],
        compiler_params=pltpu.CompilerParams(
            collective_id=0, has_side_effects=True, vmem_limit_bytes=64 * 2**20
        ),
    )(owner_table, bias_vector, *operands, dense_weights)
    results = (
        (field, BF16),
        (field, BF16),
        ((1,) + dense, F32),
        ((R, C), F32),
        ((R, C), F32),
        ((2, R, K1), F32),
        ((R, K2), F32),
        ((K3, R), F32),
        ((C, C), F32),
        ((1, C), F32),
    )
    output, input_grad, dense_grad, in_t, out_t, first_t, second_t, third, skip, bias = pl.pallas_call(
        finish_kernel,
        out_shape=tuple(jax.ShapeDtypeStruct(*result) for result in results),
        in_specs=[vmem, vmem, vmem] + [hbm] * 4,
        out_specs=(hbm,) * len(results),
        scratch_shapes=[
            pltpu.VMEM(three_t.shape, BF16),
            pltpu.VMEM(field, BF16),
            pltpu.VMEM((1,) + dense, F32),
            pltpu.VMEM(field, BF16),
            pltpu.VMEM(field, BF16),
            pltpu.VMEM((ROWS, CG * N1, 256), BF16),
            pltpu.VMEM((NS * 32, 128), F32),
        ]
        + [pltpu.VMEM(*result) for result in results[3:]]
        + [pltpu.SemaphoreType.DMA((16,))],
        compiler_params=pltpu.CompilerParams(vmem_limit_bytes=64 * 2**20),
    )(received, packed, one_t, three_t, skip_part, output, dense_grad)
    return (
        output.reshape(inputs.shape),
        input_grad.reshape(inputs.shape),
        dense_grad,
        in_t.T,
        out_t.T,
        jnp.swapaxes(first_t, 1, 2),
        second_t.T,
        third,
        skip,
        bias.reshape(C),
    )


def solution(mesh):
    field = P("batch", "space", None, None, None)
    dense = P("space", "batch", None, None, None)
    whole = P()
    return jax.shard_map(
        local,
        mesh=mesh,
        in_specs=(field, field, dense, whole, P("space", None, None)) + (whole,) * 7,
        out_specs=(field, field, dense) + (whole,) * 7,
        check_vma=False,
    )
```

profile of v0, /device:TPU:1, one launch (start us, length us, event | category | flops | bytes accessed | tf_op | source)
XLA Modules:
  0.0 84.7 jit_solution(12134626278972666640)
XLA Ops:
  0.6 77.3 %shard_map.276 = (bf16[2,8,8,64,128]{4,3,2,1,0:T(8,128)(2,1)}, bf16[2,8,8,64,128]{4,3,2,1,0:T(8,128)(2,1)}, f32[1,2,16,64,128]{4,3,2,1,0:T(8,128)}, bf16[32,32,128]{2,1,0:T(8,128)(2,1)}, f32[64,128]{1,0:T(8,128)}) custom-call(s32[16]{0:T(128)} %owner_ref.1, f32[64]{0:T(128)} %bias_ref.1, bf16[2,8,8,64,128]{4,3,2,1,0:T(8,128)(2,1)} %bitcast.13, ...), custom_call_target="tpu_custom_call" | custom-call | tf_op jit(solution)/shard_map/pallas_call | solution.py:862
  77.9 6.8 %shard_map.277 = (bf16[2,8,8,64,128]{4,3,2,1,0:T(8,128)(2,1)}, bf16[2,8,8,64,128]{4,3,2,1,0:T(8,128)(2,1)}, f32[1,2,16,64,128]{4,3,2,1,0:T(8,128)}, f32[16,64]{1...) custom-call(bf16[32,32,128]{2,1,0:T(8,128)(2,1)} %get-tuple-element., ...), custom_call_target="tpu_custom_call" | custom-call | tf_op jit(solution)/shard_map/pallas_call | solution.py:930
where the time goes:
time: 86.2 us; the launch traced here: 84.7 us
  Pallas kernels  84 us (97%)
    pallas_call x1, Pallas kernels, local(): pl.pallas_call(kernel, out_shape=(jax.ShapeDtypeStruct(field, BF16), jax....  77.3 us
    pallas_call x1, Pallas kernels, local(): pl.pallas_call(finish_kernel, out_shape=tuple((jax.ShapeDtypeStruct(*resu...  6.77 us

commit v1 on v0

--- a/solution.py
+++ b/solution.py
@@ -30,6 +30,7 @@
 CG = 8
 CQ = 8
 SLOTS = L2 // NB
+HALF = NS * 16
 GRAD_SCALE = float(SAMPLES * N1 * N2 * N3) ** (-0.5)
 
 
@@ -60,7 +61,7 @@
     two[0, :, :, 1] = sin2
     two[1, :, :, 0] = -sin2
     two[1, :, :, 1] = cos2
-    two = two.reshape(2 * K2, 2 * N2)
+    two = two.reshape(2, K2, NS, ROWS, 2).transpose(0, 1, 3, 2, 4).reshape(2 * K2, 2 * N2)
     cos3, sin3 = twiddles(np.arange(K3), N3)
     three = np.zeros((CQ, N3, 2, K3, CQ), np.float32)
     for q in range(CQ):
@@ -144,35 +145,35 @@
     pltpu.make_async_copy(block, block, sem).wait()
 
 
-def backward_rows(blocks, zf, left_v, one_t):
-    zf[...] = blocks.reshape(NS * 32, 128).astype(F32)
-    for n in range(ROWS):
-        block = jnp.concatenate(
-            [
-                jnp.concatenate(
-                    [
-                        zf[pl.ds(n * 16 + part * 8 + g, K1, stride=32), :].astype(BF16)
-                        for part in range(2)
-                    ],
-                    axis=0,
-                )
-                for g in range(CG)
-            ],
-            axis=1,
-        )
-        field = dot(one_t, block).astype(BF16)
-        for g in range(CG):
-            left_v[n, g * N1 : (g + 1) * N1, :128] = field[:N1, g * 128 : (g + 1) * 128]
-            left_v[n, g * N1 : (g + 1) * N1, 128:] = field[N1:, g * 128 : (g + 1) * 128]
-
-
-def each_pair(n, left_v, three_t, body):
-    @pl.loop(0, CQ // 2)
+def backward_row(blocks, zf, left_v, one_t):
+    zf[...] = blocks.reshape(HALF, 128).astype(F32)
+    block = jnp.concatenate(
+        [
+            jnp.concatenate(
+                [zf[pl.ds(part * 8 + g, K1, stride=16), :].astype(BF16) for part in range(2)],
+                axis=0,
+            )
+            for g in range(CG)
+        ],
+        axis=1,
+    )
+    field = dot(one_t, block).astype(BF16)
+    for g in range(CG):
+        left_v[g * N1 : (g + 1) * N1, :128] = field[:N1, g * 128 : (g + 1) * 128]
+        left_v[g * N1 : (g + 1) * N1, 128:] = field[N1:, g * 128 : (g + 1) * 128]
+
+
+def each_pair(left_v, three_t, body, after=None):
+    @pl.loop(0, CQ // 2, unroll=4)
     def _(pair):
         column = pl.multiple_of(pair * 256, 256)
-        field = dot(left_v[n], three_t[:, pl.ds(column, 256)])
-        for half in range(2):
+        field = dot(left_v[...], three_t[:, pl.ds(column, 256)])
+        made = [
             body(pair * 2 + half, field[:, half * 128 : (half + 1) * 128].reshape(CG, N1, N3))
+            for half in range(2)
+        ]
+        if after is not None:
+            after(column, jnp.concatenate([v.reshape(CG * N1, N3) for v in made], axis=1))
 
 
 def kernel(
@@ -199,9 +200,10 @@
     w_hbm,
     out_hbm,
     skip_out_hbm,
+    ig_hbm,
     dg_hbm,
-    blocks_ref,
-    red_ref,
+    blocks_hbm,
+    red_hbm,
     x_ref,
     three_ref,
     one_ref,
@@ -225,8 +227,11 @@
     gp_v,
     dg_v,
     skip_v,
+    ig_v,
     kron_v,
+    kron_back_v,
     left_v,
+    total_v,
     zf,
     sbuf,
     rbuf,
@@ -241,6 +246,8 @@
     fac_v,
     xs,
     bz,
+    lefts_v,
+    grads_v,
     sgs,
     pk,
     r_batch,
@@ -266,9 +273,34 @@
         copy.start()
         return copy
 
-    x_copies = [fetch(x_hbm.at[n], x_ref.at[n], n) for n in range(ROWS)]
+    x_copies = [fetch(x_hbm.at[0], x_ref.at[0], 0)]
     three_copy = fetch(three_hbm, three_ref, 2)
     one_copy = fetch(one_hbm, one_ref, 3)
+    x_copies.append(fetch(x_hbm.at[1], x_ref.at[1], 1))
+    barrier = pltpu.get_barrier_semaphore()
+
+    def each_space_peer(body):
+        for step in (2, 1, 3, 0):
+
+            @pl.loop(0 if step else 1, 8)
+            def _(d):
+                body(
+                    lax.rem(me_s // 8 + d // 2, 4) * 8
+                    + lax.rem(me_s // 2 + step, 4) * 2
+                    + lax.rem(me_s + d, 2)
+                )
+
+    def greet(peer):
+        pl.semaphore_signal(barrier, inc=1, device_id={"space": peer}, device_id_type=MESH)
+
+    each_space_peer(greet)
+
+    @pl.loop(1, NB)
+    def _(d):
+        pl.semaphore_signal(
+            barrier, inc=1, device_id={"batch": lax.rem(me_b + d, NB)}, device_id_type=MESH
+        )
+
     small_copies = [
         fetch(src, dst, 4 + index)
         for index, (src, dst) in enumerate(
@@ -293,37 +325,22 @@
     cot_copy = fetch(cot_hbm, cot_v, 18)
     w_copy = fetch(w_hbm.at[0], w_v, 19)
 
-    barrier = pltpu.get_barrier_semaphore()
-
-    @pl.loop(1, NS)
-    def _(d):
-        pl.semaphore_signal(
-            barrier, inc=1, device_id={"space": lax.rem(me_s + d, NS)}, device_id_type=MESH
-        )
-
-    @pl.loop(1, NB)
-    def _(d):
-        pl.semaphore_signal(
-            barrier, inc=1, device_id={"batch": lax.rem(me_b + d, NB)}, device_id_type=MESH
-        )
-
-    def space_start(phase):
-        @pl.loop(1, NS)
-        def _(d):
-            peer = lax.rem(me_s + d, NS)
+    def space_start(index):
+        def send_block(peer):
             pltpu.make_async_remote_copy(
-                src_ref=sbuf.at[phase, peer],
-                dst_ref=rbuf.at[phase, me_s],
-                send_sem=ssend.at[phase],
-                recv_sem=srecv.at[phase],
+                src_ref=sbuf.at[index, peer],
+                dst_ref=rbuf.at[index, me_s],
+                send_sem=ssend.at[index],
+                recv_sem=srecv.at[index],
                 device_id={"space": peer},
                 device_id_type=MESH,
             ).start()
 
-        rbuf[phase, me_s] = sbuf[phase, me_s]
-
-    def space_wait(phase):
-        drain(rbuf.at[phase, pl.ds(0, NS - 1)], srecv.at[phase])
+        each_space_peer(send_block)
+        rbuf[index, me_s] = sbuf[index, me_s]
+
+    def space_wait(index):
+        drain(rbuf.at[index, pl.ds(0, NS - 1)], srecv.at[index])
 
     def batch_start(phase):
         @pl.loop(1, NB)
@@ -343,37 +360,40 @@
     def batch_wait(phase):
         drain(brecv.at[phase, pl.ds(0, NB - 1)], brsem.at[phase])
 
-    def forward_cells(src, phase, copies):
+    def forward_row(src, n, index):
+        total = None
+        for q in range(0, CQ, 2):
+            pair = jnp.concatenate(
+                [src[n, :, q].reshape(CG * N1, N3), src[n, :, q + 1].reshape(CG * N1, N3)], axis=1
+            )
+            term = dot(pair, three_ref[q * N3 : (q + 2) * N3, :])
+            total = term if total is None else total + term
+        send_row(total, n, index)
+
+    def send_row(total, n, index):
+        total = total.astype(BF16)
+        right = jnp.concatenate(
+            [
+                jnp.concatenate(
+                    [total[g * N1 : (g + 1) * N1, :128], total[g * N1 : (g + 1) * N1, 128:]], axis=0
+                )
+                for g in range(CG)
+            ],
+            axis=1,
+        )
+        modes = dot(one_ref[...], right)
+        for g in range(CG):
+            for part in range(2):
+                zf[pl.ds(n * HALF + part * 8 + g, K1, stride=16), :] = modes[
+                    part * K1 : (part + 1) * K1, g * 128 : (g + 1) * 128
+                ]
+        sbuf[index] = zf[n * HALF : (n + 1) * HALF, :].astype(BF16).reshape(NS, 16, 128)
+        space_start(index)
+
+    def modes_in(phase, table):
         for n in range(ROWS):
-            if copies is not None:
-                copies[n].wait()
-            total = None
-            for q in range(0, CQ, 2):
-                pair = jnp.concatenate(
-                    [src[n, :, q].reshape(CG * N1, N3), src[n, :, q + 1].reshape(CG * N1, N3)], axis=1
-                )
-                term = dot(pair, three_ref[q * N3 : (q + 2) * N3, :])
-                total = term if total is None else total + term
-            total = total.astype(BF16)
-            right = jnp.concatenate(
-                [
-                    jnp.concatenate(
-                        [total[g * N1 : (g + 1) * N1, :128], total[g * N1 : (g + 1) * N1, 128:]], axis=0
-                    )
-                    for g in range(CG)
-                ],
-                axis=1,
-            )
-            modes = dot(one_ref[...], right)
-            for g in range(CG):
-                for part in range(2):
-                    zf[pl.ds(n * 16 + part * 8 + g, K1, stride=32), :] = modes[
-                        part * K1 : (part + 1) * K1, g * 128 : (g + 1) * 128
-                    ]
-        sbuf[phase] = zf[...].astype(BF16).reshape(NS, 32, 128)
-
-    def modes_in(phase, table):
-        zf[...] = rbuf[phase].reshape(NS * 32, 128).astype(F32)
+            space_wait(2 * phase + n)
+            zf[n * HALF : (n + 1) * HALF, :] = rbuf[2 * phase + n].reshape(HALF, 128).astype(F32)
         cells = jnp.concatenate(
             [zf[pl.ds(g, 2 * N2, stride=8), :].astype(BF16) for g in range(CG)], axis=1
         )
@@ -394,19 +414,23 @@
             ],
             axis=0,
         )
-        cells = dot(table, spectrum)
-        for g in range(CG):
-            zf[pl.ds(g, 2 * N2, stride=8), :] = cells[:, g * 128 : (g + 1) * 128]
-        sbuf[phase] = zf[...].astype(BF16).reshape(NS, 32, 128)
-
-    def mix_channels(src, with_bias):
+        for n in range(ROWS):
+            cells = dot(table[n * N2 : (n + 1) * N2], spectrum)
+            for g in range(CG):
+                zf[pl.ds(n * HALF + g, N2, stride=8), :] = cells[:, g * 128 : (g + 1) * 128]
+            sbuf[2 * phase + n] = (
+                zf[n * HALF : (n + 1) * HALF, :].astype(BF16).reshape(NS, 16, 128)
+            )
+            space_start(2 * phase + n)
+
+    def mix_channels(src, kron, with_bias):
         @pl.loop(0, N1 // 16)
         def _(step):
             cut = pl.ds(pl.multiple_of(step * 16, 16), 16)
             right = jnp.concatenate(
                 [src[n, :, :, cut, :].reshape(C * 16, N3) for n in range(ROWS)], axis=1
             )
-            mixed = dot(kron_v[...], right)
+            mixed = dot(kron[...], right)
             for n in range(ROWS):
                 value = mixed[:, n * N3 : (n + 1) * N3].reshape(C, 16, N3)
                 if with_bias:
@@ -416,19 +440,21 @@
     spread_rows = (rows((C * 16, C)) // 16 == lanes((C * 16, C))).astype(F32)
     spread_half = spread_rows.astype(BF16)
 
-    def build_kron(base):
+    def build_kron(base, kron):
         expanded = dot(spread_half, base).astype(BF16)
         for block in range(4):
             cut = slice(block * 256, (block + 1) * 256)
             full = dot_nt(expanded[cut], spread_half)
             same = (rows((256, 1024)) & 15) == (lanes((256, 1024)) & 15)
-            kron_v[cut, :] = jnp.where(same, full, 0.0).astype(BF16)
+            kron[cut, :] = jnp.where(same, full, 0.0).astype(BF16)
 
     three_copy.wait()
     one_copy.wait()
-    forward_cells(x_ref, 0, x_copies)
-    pl.semaphore_wait(barrier, NS - 1 + NB - 1)
-    space_start(0)
+    for n in range(ROWS):
+        x_copies[n].wait()
+        if n == 0:
+            pl.semaphore_wait(barrier, NS - 1 + NB - 1)
+        forward_row(x_ref, n, n)
 
     for copy in small_copies:
         copy.wait()
@@ -472,10 +498,10 @@
     fout_b = expand(fout_ref[...], 1, 3, 128)
     fout_c = expand(fout_ref[...], 4, 5, 128)
 
-    build_kron(skip_ref[...].astype(F32).T.astype(BF16))
-    mix_channels(x_ref, True)
-
-    space_wait(0)
+    build_kron(skip_ref[...].astype(F32).T.astype(BF16), kron_v)
+    mix_channels(x_ref, kron_v, True)
+    build_kron(skip_ref[...], kron_back_v)
+
     spectrum = modes_in(0, two)
     for k in range(K3):
         sm[k * K2 : (k + 1) * K2, :] = spectrum[k]
@@ -506,8 +532,9 @@
     for index in range(SLOTS * K3):
         slot, k = divmod(index, K3)
         value = xs[pl.ds(index, NB, stride=32), :]
-        left = jnp.concatenate([value, pltpu.roll(value, 64, 1)], axis=0)[:, :C].astype(BF16)
-        both = dot(left, w_v[slot, k])
+        left = jnp.concatenate([value, pltpu.roll(value, 64, 1)], axis=0).astype(BF16)
+        lefts_v[index] = left
+        both = dot(left[:, :C], w_v[slot, k])
         bz[pl.ds(index, NB, stride=32), :] = both[:8] + sign * pltpu.roll(both[8:], 64, 1)
     bsend[1] = bz[...].astype(BF16).reshape(NB, 32, 128)
     batch_start(1)
@@ -520,12 +547,11 @@
         )
         out_spec.append(jnp.concatenate([low, fac_v[k * K2 + L2 : (k + 1) * K2, :]], axis=0))
     modes_out(out_spec, two_t, 1)
-    space_start(1)
     cot_copy.wait()
-    space_wait(1)
-    backward_rows(rbuf[1], zf, left_v, one_t_ref[...])
 
     for n in range(ROWS):
+        space_wait(2 + n)
+        backward_row(rbuf[2 + n], zf.at[pl.ds(n * HALF, HALF)], left_v, one_t_ref[...])
 
         def activate(q, field):
             v = field + skip_v[n, :, q].astype(F32)
@@ -535,19 +561,19 @@
             active = v * gate
             out_v[n, :, q] = active.astype(BF16)
             slope = gate + active * (1.0 - gate) * (2.0 * k0 + (6.0 * k0 * 0.044715) * square)
-            gp_v[n, :, q] = (cot_v[n, :, q].astype(F32) * slope).astype(BF16)
-
-        each_pair(n, left_v, three_t_ref, activate)
+            made = (cot_v[n, :, q].astype(F32) * slope).astype(BF16)
+            gp_v[n, :, q] = made
+            return made
+
+        def gather(column, pair):
+            total_v[...] += dot(pair, three_ref[pl.ds(column, 256), :])
+
+        total_v[...] = jnp.zeros_like(total_v)
+        each_pair(left_v, three_t_ref, activate, gather)
+        send_row(total_v[...], n, 4 + n)
     out_copy = pltpu.make_async_copy(out_v, out_hbm, out_sem.at[0])
     out_copy.start()
 
-    forward_cells(gp_v, 2, None)
-    space_start(2)
-
-    build_kron(skip_ref[...])
-    mix_channels(gp_v, False)
-    skip_copy = pltpu.make_async_copy(skip_v, skip_out_hbm, out_sem.at[2])
-    skip_copy.start()
     same = ((rows((16, 256)) & 15) == (lanes((16, 256)) & 15)).astype(F32)
     ones = jnp.ones((16, ROWS * 4 * N3), BF16)
 
@@ -573,7 +599,6 @@
 
     skip_grad = dot(sgs[...], spread_rows, HIGH)
 
-    space_wait(2)
     grad_spec = modes_in(2, two)
     cold = []
     for k in range(K3):
@@ -661,16 +686,17 @@
     bz[...] = brecv[2].reshape(NB * 32, 128).astype(F32)
     for index in range(SLOTS * K3):
         slot, k = divmod(index, K3)
-        value = xs[pl.ds(index, NB, stride=32), :]
         grad = bz[pl.ds(index, NB, stride=32), :]
-        left = jnp.concatenate([value, pltpu.roll(value, 64, 1)], axis=0).astype(BF16)
         grads = jnp.concatenate([grad, -sign * pltpu.roll(grad, 64, 1)], axis=0).astype(BF16)
+        grads_v[index] = grads
         weights = w_v[slot, k]
         both = dot_nt(grads, jnp.concatenate([weights, weights], axis=0))
         bz[pl.ds(index, NB, stride=32), :] = jnp.where(sign < 0.0, both[:8], both[8:])
-        dg_v[slot, k] = dot_tn(left, grads)[:C]
     bsend[3] = bz[...].astype(BF16).reshape(NB, 32, 128)
     batch_start(3)
+    for index in range(SLOTS * K3):
+        slot, k = divmod(index, K3)
+        dg_v[slot, k] = dot_tn(lefts_v[index], grads_v[index])[:C]
     dg_copy = pltpu.make_async_copy(dg_v, dg_hbm.at[0], out_sem.at[1])
     dg_copy.start()
 
@@ -684,6 +710,10 @@
         send(part_near, r_near.at[near], 1, {"space": peer})
 
     r_near[near] = part_near[...]
+
+    mix_channels(gp_v, kron_back_v, False)
+    skip_copy = pltpu.make_async_copy(skip_v, skip_out_hbm, out_sem.at[2])
+    skip_copy.start()
 
     batch_wait(3)
     slots_in(3)
@@ -694,7 +724,6 @@
             jnp.concatenate([low, fac_v[k * K2 + L2 : (k + 1) * K2, :]], axis=0)
         )
     modes_out(grad_spectrum, two_t, 3)
-    space_start(3)
 
 
     drain(r_near.at[pl.ds(0, 7)], rrecv.at[1])
@@ -707,6 +736,17 @@
         send(part_far, r_far.at[far], 2, {"space": peer})
 
     r_far[far] = part_far[...]
+
+    space_wait(6)
+    backward_row(rbuf[6], zf.at[pl.ds(0, HALF)], left_v, one_t_ref[...])
+
+    def finish(q, field):
+        ig_v[:, q] = (field + skip_v[0, :, q].astype(F32)).astype(BF16)
+
+    each_pair(left_v, three_t_ref, finish)
+    ig_copy = pltpu.make_async_copy(ig_v, ig_hbm, out_sem.at[3])
+    ig_copy.start()
+
     drain(r_far.at[pl.ds(0, 3)], rrecv.at[2])
     part_all[...] = jnp.sum(r_far[...], axis=0)
 
@@ -715,31 +755,33 @@
         send(part_all, r_all.at[me_b], 3, {"batch": lax.rem(me_b + d, NB)})
 
     r_all[me_b] = part_all[...]
+    space_wait(7)
+    blocks_copy = pltpu.make_async_copy(rbuf.at[7], blocks_hbm, out_sem.at[4])
+    blocks_copy.start()
     drain(r_all.at[pl.ds(0, NB - 1)], rrecv.at[3])
-    red_ref[...] = r_all[...].reshape(C, 128)
-
-    space_wait(3)
-    blocks_ref[...] = rbuf[3]
+    red_copy = pltpu.make_async_copy(r_all, red_hbm, out_sem.at[5])
+    red_copy.start()
+    for index in range(8):
+        drain(sbuf.at[index, pl.ds(0, NS - 1)], ssend.at[index])
     for phase in range(4):
-        drain(sbuf.at[phase, pl.ds(0, NS - 1)], ssend.at[phase])
         drain(bsend.at[phase, pl.ds(0, NB - 1)], bssem.at[phase])
     drain(pk.at[pl.ds(0, NB - 1)], rsend.at[0])
     drain(r_near.at[pl.ds(0, 7)], rsend.at[1])
     drain(r_far.at[pl.ds(0, 3)], rsend.at[2])
     drain(r_all.at[pl.ds(0, NB - 1)], rsend.at[3])
-    out_copy.wait()
-    dg_copy.wait()
-    skip_copy.wait()
+    for started in (out_copy, dg_copy, skip_copy, ig_copy, blocks_copy, red_copy):
+        started.wait()
 
 
 def finish_kernel(
-    blocks_ref,
-    packed_ref,
-    one_t_ref,
+    blocks_hbm,
+    packed_hbm,
+    one_t_hbm,
     three_t_hbm,
     skip_hbm,
     out_in,
     dg_in,
+    ig_in,
     out_hbm,
     ig_hbm,
     dg_hbm,
@@ -750,10 +792,13 @@
     third_hbm,
     mix_hbm,
     bias_hbm,
+    blocks_v,
+    packed_v,
+    one_t_v,
     three_t_v,
+    skip_v,
     out_v,
     dg_v,
-    skip_v,
     ig_v,
     left_v,
     zf,
@@ -771,11 +816,32 @@
         started.start()
         return started
 
-    three_copy = copy(three_t_hbm, three_t_v, 2)
-    skip_copies = [copy(skip_hbm.at[n], skip_v.at[n], n) for n in range(ROWS)]
-    moved_in = [copy(out_in, out_v, 3), copy(dg_in, dg_v, 4)]
-    backward_rows(blocks_ref[...], zf, left_v, one_t_ref[...])
-    packed = packed_ref[...]
+    arriving = [
+        copy(src, dst, index)
+        for index, (src, dst) in enumerate(
+            (
+                (blocks_hbm, blocks_v),
+                (one_t_hbm, one_t_v),
+                (three_t_hbm, three_t_v),
+                (skip_hbm.at[1], skip_v),
+                (packed_hbm, packed_v),
+                (out_in, out_v),
+                (ig_in, ig_v.at[0]),
+                (dg_in, dg_v),
+            )
+        )
+    ]
+    waits = []
+
+    def pass_on(index, src, dst):
+        arriving[index].wait()
+        waits.append(copy(src, dst, 8 + index))
+
+    for index in range(4):
+        arriving[index].wait()
+    backward_row(blocks_v[...], zf, left_v, one_t_v[...])
+    arriving[4].wait()
+    packed = packed_v[...].reshape(C, 128)
     turned = packed.T
     fin_v[...] = turned[64:80]
     fout_v[...] = turned[80:96]
@@ -799,19 +865,21 @@
         (mix_v, mix_hbm),
         (bias_v, bias_hbm),
     )
-    waits = [copy(src, dst, 5 + index) for index, (src, dst) in enumerate(small)]
-    for arrived in moved_in:
-        arrived.wait()
-    waits += [copy(out_v, out_hbm, 14), copy(dg_v, dg_hbm, 15)]
-    three_copy.wait()
-    for n in range(ROWS):
-        skip_copies[n].wait()
-
-        def finish(q, field):
-            ig_v[n, :, q] = (field + skip_v[n, :, q].astype(F32)).astype(BF16)
-
-        each_pair(n, left_v, three_t_v, finish)
-        waits.append(copy(ig_v.at[n], ig_hbm.at[n], 12 + n))
+    waits += [copy(src, dst, 17 + index) for index, (src, dst) in enumerate(small)]
+    for pair in range(CQ // 2):
+        field = dot(left_v[...], three_t_v[:, pair * 256 : (pair + 1) * 256])
+        for half in range(2):
+            q = pair * 2 + half
+            value = field[:, half * 128 : (half + 1) * 128].reshape(CG, N1, N3)
+            ig_v[1, :, q] = (value + skip_v[:, q].astype(F32)).astype(BF16)
+        cut = (1, slice(None), pl.ds(pair * 2, 2))
+        waits.append(copy(ig_v.at[cut], ig_hbm.at[cut], 24 + pair))
+        if pair == 0:
+            pass_on(5, out_v, out_hbm)
+        if pair == 1:
+            pass_on(6, ig_v.at[0], ig_hbm.at[0])
+        if pair == 2:
+            pass_on(7, dg_v, dg_hbm)
     for started in waits:
         started.wait()
 
@@ -834,7 +902,6 @@
     three, three_t, one, one_t, two, two_t, patterns, spread, select = [
         jnp.asarray(table) for table in build_tables()
     ]
-    vmem = pl.BlockSpec(memory_space=pltpu.VMEM)
     smem = pl.BlockSpec(memory_space=pltpu.SMEM)
     hbm = pl.BlockSpec(memory_space=pltpu.HBM)
     dense = (SLOTS, K3, C, 2 * C)
@@ -858,18 +925,20 @@
         three_t,
         cotangent.reshape(field),
     )
-    blocks = (NS, 32, 128)
-    output, skip_part, dense_grad, received, packed = pl.pallas_call(
+    blocks = (NS, 16, 128)
+    row = field[1:]
+    output, skip_part, grad_row, dense_grad, received, packed = pl.pallas_call(
         kernel,
         out_shape=(
             jax.ShapeDtypeStruct(field, BF16),
             jax.ShapeDtypeStruct(field, BF16),
+            jax.ShapeDtypeStruct(row, BF16),
             jax.ShapeDtypeStruct((1,) + dense, F32),
             jax.ShapeDtypeStruct(blocks, BF16),
-            jax.ShapeDtypeStruct((C, 128), F32),
+            jax.ShapeDtypeStruct((NB, 8, 128), F32),
         ),
         in_specs=[smem, smem] + [hbm] * 19,
-        out_specs=(hbm, hbm, hbm, vmem, vmem),
+        out_specs=(hbm,) * 6,
         scratch_shapes=[pltpu.VMEM(value.shape, value.dtype) for value in operands]
         + [
             pltpu.VMEM(dense, BF16),
@@ -877,11 +946,14 @@
             pltpu.VMEM(field, BF16),
             pltpu.VMEM(dense, F32),
             pltpu.VMEM(field, BF16),
+            pltpu.VMEM(row, BF16),
             pltpu.VMEM((C * 16, C * 16), BF16),
-            pltpu.VMEM((ROWS, CG * N1, 256), BF16),
-            pltpu.VMEM((NS * 32, 128), F32),
-            pltpu.VMEM((4,) + blocks, BF16),
-            pltpu.VMEM((4,) + blocks, BF16),
+            pltpu.VMEM((C * 16, C * 16), BF16),
+            pltpu.VMEM((CG * N1, 256), BF16),
+            pltpu.VMEM((CG * N1, 256), F32),
+            pltpu.VMEM((ROWS * HALF, 128), F32),
+            pltpu.VMEM((8,) + blocks, BF16),
+            pltpu.VMEM((8,) + blocks, BF16),
             pltpu.VMEM((4, NB, 32, 128), BF16),
             pltpu.VMEM((4, NB, 32, 128), BF16),
             pltpu.VMEM((K3 * K2, 128), F32),
@@ -893,6 +965,8 @@
             pltpu.VMEM((K3 * K2, 128), F32),
             pltpu.VMEM((NB * 32, 128), F32),
             pltpu.VMEM((NB * 32, 128), F32),
+            pltpu.VMEM((SLOTS * K3, 16, 128), BF16),
+            pltpu.VMEM((SLOTS * K3, 16, 128), BF16),
             pltpu.VMEM((C + 16, C * 16), F32),
             pltpu.VMEM((NB, 8, 128), F32),
             pltpu.VMEM((NB, 8, 128), F32),
@@ -903,9 +977,9 @@
             pltpu.VMEM((8, 128), F32),
             pltpu.VMEM((8, 128), F32),
             pltpu.SemaphoreType.DMA((20,)),
-            pltpu.SemaphoreType.DMA((3,)),
-            pltpu.SemaphoreType.DMA((4,)),
-            pltpu.SemaphoreType.DMA((4,)),
+            pltpu.SemaphoreType.DMA((6,)),
+            pltpu.SemaphoreType.DMA((8,)),
+            pltpu.SemaphoreType.DMA((8,)),
             pltpu.SemaphoreType.DMA((4,)),
             pltpu.SemaphoreType.DMA((4,)),
             pltpu.SemaphoreType.DMA((4,)),
@@ -930,21 +1004,24 @@
     output, input_grad, dense_grad, in_t, out_t, first_t, second_t, third, skip, bias = pl.pallas_call(
         finish_kernel,
         out_shape=tuple(jax.ShapeDtypeStruct(*result) for result in results),
-        in_specs=[vmem, vmem, vmem] + [hbm] * 4,
+        in_specs=[hbm] * 8,
         out_specs=(hbm,) * len(results),
         scratch_shapes=[
+            pltpu.VMEM(blocks, BF16),
+            pltpu.VMEM((NB, 8, 128), F32),
+            pltpu.VMEM(one_t.shape, BF16),
             pltpu.VMEM(three_t.shape, BF16),
+            pltpu.VMEM(row, BF16),
             pltpu.VMEM(field, BF16),
             pltpu.VMEM((1,) + dense, F32),
             pltpu.VMEM(field, BF16),
-            pltpu.VMEM(field, BF16),
-            pltpu.VMEM((ROWS, CG * N1, 256), BF16),
-            pltpu.VMEM((NS * 32, 128), F32),
+            pltpu.VMEM((CG * N1, 256), BF16),
+            pltpu.VMEM((HALF, 128), F32),
         ]
         + [pltpu.VMEM(*result) for result in results[3:]]
-        + [pltpu.SemaphoreType.DMA((16,))],
+        + [pltpu.SemaphoreType.DMA((28,))],
         compiler_params=pltpu.CompilerParams(vmem_limit_bytes=64 * 2**20),
-    )(received, packed, one_t, three_t, skip_part, output, dense_grad)
+    )(received, packed, one_t, three_t, skip_part, output, dense_grad, grad_row)
     return (
         output.reshape(inputs.shape),
         input_grad.reshape(inputs.shape),

time: 86.2 us -> 80.5 us (0.934); the launches traced: 84.7 us -> 80.4 us
  Pallas kernels: 84 us -> 79.6 us
    pallas_call x1, Pallas kernels: 77.3 us -> 74.9 us  [local(): pl.pallas_call(kernel, out_shape=(jax.ShapeDtypeStruct(field, BF16), jax....]
    pallas_call x1, Pallas kernels: 6.77 us -> 4.69 us  [local(): pl.pallas_call(finish_kernel, out_shape=tuple((jax.ShapeDtypeStruct(*resu...]
where the time goes in v1:
time: 80.5 us; the launch traced here: 80.4 us
  Pallas kernels  79.6 us (99%)
  between operations  0.82 us (1%)
    pallas_call x1, Pallas kernels, local(): pl.pallas_call(kernel, out_shape=(jax.ShapeDtypeStruct(field, BF16), jax....  74.9 us
    pallas_call x1, Pallas kernels, local(): pl.pallas_call(finish_kernel, out_shape=tuple((jax.ShapeDtypeStruct(*resu...  4.69 us

profile of v1, /device:TPU:1, one launch (start us, length us, event | category | flops | bytes accessed | tf_op | source)
XLA Modules:
  0.0 80.4 jit_solution(18403862026341159249)
XLA Ops:
  0.6 74.9 %shard_map.276 = (bf16[2,8,8,64,128]{4,3,2,1,0:T(8,128)(2,1)}, bf16[2,8,8,64,128]{4,3,2,1,0:T(8,128)(2,1)}, bf16[8,8,64,128]{3,2,1,0:T(8,128)(2,1)}, f32[1,2,16,...) custom-call(s32[16]{0:T(128)} %owner_ref.1, f32[64]{0:T(128)} %bias_ref.1, ...), custom_call_target="tpu_custom_call" | custom-call | tf_op jit(solution)/shard_map/pallas_call | solution.py:930
  75.6 4.7 %shard_map.277 = (bf16[2,8,8,64,128]{4,3,2,1,0:T(8,128)(2,1)}, bf16[2,8,8,64,128]{4,3,2,1,0:T(8,128)(2,1)}, f32[1,2,16,64,128]{4,3,2,1,0:T(8,128)}, f32[16,64]{1...) custom-call(bf16[32,16,128]{2,1,0:T(8,128)(2,1)} %get-tuple-element., ...), custom_call_target="tpu_custom_call" | custom-call | tf_op jit(solution)/shard_map/pallas_call | solution.py:1004

commit v2 on v1

--- a/solution.py
+++ b/solution.py
@@ -295,11 +295,14 @@
 
     each_space_peer(greet)
 
-    @pl.loop(1, NB)
-    def _(d):
-        pl.semaphore_signal(
-            barrier, inc=1, device_id={"batch": lax.rem(me_b + d, NB)}, device_id_type=MESH
-        )
+    def each_batch_peer(body):
+        for z_step, y_step in ((1, 2), (1, 1), (1, 3), (0, 2), (1, 0), (0, 1), (0, 3)):
+            body(lax.rem(me_b // 4 + z_step, 2) * 4 + lax.rem(me_b + y_step, 4))
+
+    def greet_batch(peer):
+        pl.semaphore_signal(barrier, inc=1, device_id={"batch": peer}, device_id_type=MESH)
+
+    each_batch_peer(greet_batch)
 
     small_copies = [
         fetch(src, dst, 4 + index)
@@ -343,9 +346,7 @@
         drain(rbuf.at[index, pl.ds(0, NS - 1)], srecv.at[index])
 
     def batch_start(phase):
-        @pl.loop(1, NB)
-        def _(d):
-            peer = lax.rem(me_b + d, NB)
+        def send_block(peer):
             pltpu.make_async_remote_copy(
                 src_ref=bsend.at[phase, peer],
                 dst_ref=brecv.at[phase, me_b],
@@ -355,6 +356,7 @@
                 device_id_type=MESH,
             ).start()
 
+        each_batch_peer(send_block)
         brecv[phase, me_b] = bsend[phase, me_b]
 
     def batch_wait(phase):
@@ -368,9 +370,9 @@
             )
             term = dot(pair, three_ref[q * N3 : (q + 2) * N3, :])
             total = term if total is None else total + term
-        send_row(total, n, index)
-
-    def send_row(total, n, index):
+        fill_row(total, n, index)
+
+    def fill_row(total, n, index):
         total = total.astype(BF16)
         right = jnp.concatenate(
             [
@@ -388,7 +390,6 @@
                     part * K1 : (part + 1) * K1, g * 128 : (g + 1) * 128
                 ]
         sbuf[index] = zf[n * HALF : (n + 1) * HALF, :].astype(BF16).reshape(NS, 16, 128)
-        space_start(index)
 
     def modes_in(phase, table):
         for n in range(ROWS):
@@ -452,9 +453,10 @@
     one_copy.wait()
     for n in range(ROWS):
         x_copies[n].wait()
-        if n == 0:
-            pl.semaphore_wait(barrier, NS - 1 + NB - 1)
         forward_row(x_ref, n, n)
+    pl.semaphore_wait(barrier, NS - 1 + NB - 1)
+    for n in range(ROWS):
+        space_start(n)
 
     for copy in small_copies:
         copy.wait()
@@ -570,7 +572,8 @@
 
         total_v[...] = jnp.zeros_like(total_v)
         each_pair(left_v, three_t_ref, activate, gather)
-        send_row(total_v[...], n, 4 + n)
+        fill_row(total_v[...], n, 4 + n)
+        space_start(4 + n)
     out_copy = pltpu.make_async_copy(out_v, out_hbm, out_sem.at[0])
     out_copy.start()
 
@@ -694,11 +697,6 @@
         bz[pl.ds(index, NB, stride=32), :] = jnp.where(sign < 0.0, both[:8], both[8:])
     bsend[3] = bz[...].astype(BF16).reshape(NB, 32, 128)
     batch_start(3)
-    for index in range(SLOTS * K3):
-        slot, k = divmod(index, K3)
-        dg_v[slot, k] = dot_tn(lefts_v[index], grads_v[index])[:C]
-    dg_copy = pltpu.make_async_copy(dg_v, dg_hbm.at[0], out_sem.at[1])
-    dg_copy.start()
 
     drain(r_batch.at[pl.ds(0, NB - 1)], rrecv.at[0])
     part_near[...] = jnp.sum(r_batch[...], axis=0)
@@ -737,6 +735,20 @@
 
     r_far[far] = part_far[...]
 
+    for index in range(SLOTS * K3):
+        slot, k = divmod(index, K3)
+        dg_v[slot, k] = dot_tn(lefts_v[index], grads_v[index])[:C]
+    dg_copy = pltpu.make_async_copy(dg_v, dg_hbm.at[0], out_sem.at[1])
+    dg_copy.start()
+
+    drain(r_far.at[pl.ds(0, 3)], rrecv.at[2])
+    part_all[...] = jnp.sum(r_far[...], axis=0)
+
+    @pl.loop(1, NB)
+    def _(d):
+        send(part_all, r_all.at[me_b], 3, {"batch": lax.rem(me_b + d, NB)})
+
+    r_all[me_b] = part_all[...]
     space_wait(6)
     backward_row(rbuf[6], zf.at[pl.ds(0, HALF)], left_v, one_t_ref[...])
 
@@ -747,14 +759,6 @@
     ig_copy = pltpu.make_async_copy(ig_v, ig_hbm, out_sem.at[3])
     ig_copy.start()
 
-    drain(r_far.at[pl.ds(0, 3)], rrecv.at[2])
-    part_all[...] = jnp.sum(r_far[...], axis=0)
-
-    @pl.loop(1, NB)
-    def _(d):
-        send(part_all, r_all.at[me_b], 3, {"batch": lax.rem(me_b + d, NB)})
-
-    r_all[me_b] = part_all[...]
     space_wait(7)
     blocks_copy = pltpu.make_async_copy(rbuf.at[7], blocks_hbm, out_sem.at[4])
     blocks_copy.start()

time: 80.5 us -> 77.9 us (0.968); the launches traced: 80.4 us -> 76.4 us
  Pallas kernels: 79.6 us -> 75.6 us
    pallas_call x1, Pallas kernels: 74.9 us -> 70.9 us  [local(): pl.pallas_call(kernel, out_shape=(jax.ShapeDtypeStruct(field, BF16), jax....]
where the time goes in v2:
time: 77.9 us; the launch traced here: 76.4 us
  Pallas kernels  75.6 us (97%)
  between operations  0.82 us (1%)
    pallas_call x1, Pallas kernels, local(): pl.pallas_call(kernel, out_shape=(jax.ShapeDtypeStruct(field, BF16), jax....  70.9 us
    pallas_call x1, Pallas kernels, local(): pl.pallas_call(finish_kernel, out_shape=tuple((jax.ShapeDtypeStruct(*resu...  4.69 us

profile of v2, /device:TPU:1, one launch (start us, length us, event | category | flops | bytes accessed | tf_op | source)
XLA Modules:
  0.0 76.4 jit_solution(17798579748953887469)
XLA Ops:
  0.6 70.9 %shard_map.276 = (bf16[2,8,8,64,128]{4,3,2,1,0:T(8,128)(2,1)}, bf16[2,8,8,64,128]{4,3,2,1,0:T(8,128)(2,1)}, bf16[8,8,64,128]{3,2,1,0:T(8,128)(2,1)}, f32[1,2,16,...) custom-call(s32[16]{0:T(128)} %owner_ref.1, f32[64]{0:T(128)} %bias_ref.1, ...), custom_call_target="tpu_custom_call" | custom-call | tf_op jit(solution)/shard_map/pallas_call | solution.py:934
  71.5 4.7 %shard_map.277 = (bf16[2,8,8,64,128]{4,3,2,1,0:T(8,128)(2,1)}, bf16[2,8,8,64,128]{4,3,2,1,0:T(8,128)(2,1)}, f32[1,2,16,64,128]{4,3,2,1,0:T(8,128)}, f32[16,64]{1...) custom-call(bf16[32,16,128]{2,1,0:T(8,128)(2,1)} %get-tuple-element., ...), custom_call_target="tpu_custom_call" | custom-call | tf_op jit(solution)/shard_map/pallas_call | solution.py:1008

commit v3 on v2

--- a/solution.py
+++ b/solution.py
@@ -328,25 +328,29 @@
     cot_copy = fetch(cot_hbm, cot_v, 18)
     w_copy = fetch(w_hbm.at[0], w_v, 19)
 
-    def space_start(index):
+    def space_start(*indices):
         def send_block(peer):
-            pltpu.make_async_remote_copy(
-                src_ref=sbuf.at[index, peer],
-                dst_ref=rbuf.at[index, me_s],
-                send_sem=ssend.at[index],
-                recv_sem=srecv.at[index],
-                device_id={"space": peer},
-                device_id_type=MESH,
-            ).start()
+            for index in indices:
+                pltpu.make_async_remote_copy(
+                    src_ref=sbuf.at[index, peer],
+                    dst_ref=rbuf.at[index, me_s],
+                    send_sem=ssend.at[index],
+                    recv_sem=srecv.at[index],
+                    device_id={"space": peer},
+                    device_id_type=MESH,
+                ).start()
 
         each_space_peer(send_block)
-        rbuf[index, me_s] = sbuf[index, me_s]
+        for index in indices:
+            rbuf[index, me_s] = sbuf[index, me_s]
 
     def space_wait(index):
         drain(rbuf.at[index, pl.ds(0, NS - 1)], srecv.at[index])
 
-    def batch_start(phase):
+    def batch_start(phase, fill=None):
         def send_block(peer):
+            if fill is not None:
+                fill(bsend, phase, peer, peer)
             pltpu.make_async_remote_copy(
                 src_ref=bsend.at[phase, peer],
                 dst_ref=brecv.at[phase, me_b],
@@ -357,7 +361,10 @@
             ).start()
 
         each_batch_peer(send_block)
-        brecv[phase, me_b] = bsend[phase, me_b]
+        if fill is not None:
+            fill(brecv, phase, me_b, me_b)
+        else:
+            brecv[phase, me_b] = bsend[phase, me_b]
 
     def batch_wait(phase):
         drain(brecv.at[phase, pl.ds(0, NB - 1)], brsem.at[phase])
@@ -455,8 +462,7 @@
         x_copies[n].wait()
         forward_row(x_ref, n, n)
     pl.semaphore_wait(barrier, NS - 1 + NB - 1)
-    for n in range(ROWS):
-        space_start(n)
+    space_start(0, 1)
 
     for copy in small_copies:
         copy.wait()
@@ -508,20 +514,18 @@
     for k in range(K3):
         sm[k * K2 : (k + 1) * K2, :] = spectrum[k]
 
-    def slots_out(phase):
-        for owner in range(NB):
-            for slot in range(SLOTS):
-                bsend[phase, owner, slot * K3 : (slot + 1) * K3, :] = sm[
-                    pl.ds(owner * SLOTS + slot, K3, stride=K2), :
-                ].astype(BF16)
+    def slots_out(dst, phase, index, owner):
+        for slot in range(SLOTS):
+            dst[phase, index, slot * K3 : (slot + 1) * K3, :] = sm[
+                pl.ds(owner * SLOTS + slot, K3, stride=K2), :
+            ].astype(BF16)
 
     def slots_in(phase):
         bz[...] = brecv[phase].reshape(NB * 32, 128).astype(F32)
         for slot in range(L2):
             sm[pl.ds(slot, K3, stride=K2), :] = bz[slot * K3 : (slot + 1) * K3, :]
 
-    slots_out(0)
-    batch_start(0)
+    batch_start(0, slots_out)
     s16[...] = sm[...].astype(BF16)
     coef = dot(s16[...], fin_all)
     coef_b[...] = coef[:, 128:]
@@ -603,15 +607,15 @@
     skip_grad = dot(sgs[...], spread_rows, HIGH)
 
     grad_spec = modes_in(2, two)
+    for k in range(K3):
+        sm[k * K2 : k * K2 + L2, :] = grad_spec[k][:L2] * maskf[k]
+        fac_v[k * K2 : (k + 1) * K2, :] = grad_spec[k]
+    batch_start(2, slots_out)
     cold = []
     for k in range(K3):
-        low = grad_spec[k][:L2]
-        sm[k * K2 : k * K2 + L2, :] = low * maskf[k]
-        cold.append(
-            jnp.concatenate([low * (1.0 - maskf[k]), grad_spec[k][L2:]], axis=0).astype(BF16)
-        )
-    slots_out(2)
-    batch_start(2)
+        low = fac_v[k * K2 : k * K2 + L2, :] * (1.0 - maskf[k])
+        high = fac_v[k * K2 + L2 : (k + 1) * K2, :]
+        cold.append(jnp.concatenate([low, high], axis=0).astype(BF16))
     cold = jnp.concatenate(cold, axis=0)
     back = dot(cold, fout_c)
     prod_back = (back * ph[...]).astype(BF16)

time: 77.9 us -> 77.2 us (level)
  Pallas kernels: 75.6 us -> 74.8 us
where the time goes in v3:
time: 77.2 us; the launch traced here: 75.7 us
  Pallas kernels  74.8 us (97%)
  between operations  0.82 us (1%)
    pallas_call x1, Pallas kernels, local(): pl.pallas_call(kernel, out_shape=(jax.ShapeDtypeStruct(field, BF16), jax....  70.2 us
    pallas_call x1, Pallas kernels, local(): pl.pallas_call(finish_kernel, out_shape=tuple((jax.ShapeDtypeStruct(*resu...  4.69 us

profile of v3, /device:TPU:1, one launch (start us, length us, event | category | flops | bytes accessed | tf_op | source)
XLA Modules:
  0.0 75.7 jit_solution(14739894632354606877)
XLA Ops:
  0.6 70.2 %shard_map.276 = (bf16[2,8,8,64,128]{4,3,2,1,0:T(8,128)(2,1)}, bf16[2,8,8,64,128]{4,3,2,1,0:T(8,128)(2,1)}, bf16[8,8,64,128]{3,2,1,0:T(8,128)(2,1)}, f32[1,2,16,...) custom-call(s32[16]{0:T(128)} %owner_ref.1, f32[64]{0:T(128)} %bias_ref.1, ...), custom_call_target="tpu_custom_call" | custom-call | tf_op jit(solution)/shard_map/pallas_call | solution.py:938
  70.8 4.7 %shard_map.277 = (bf16[2,8,8,64,128]{4,3,2,1,0:T(8,128)(2,1)}, bf16[2,8,8,64,128]{4,3,2,1,0:T(8,128)(2,1)}, f32[1,2,16,64,128]{4,3,2,1,0:T(8,128)}, f32[16,64]{1...) custom-call(bf16[32,16,128]{2,1,0:T(8,128)(2,1)} %get-tuple-element., ...), custom_call_target="tpu_custom_call" | custom-call | tf_op jit(solution)/shard_map/pallas_call | solution.py:1012

commit v4 on v3

--- a/solution.py
+++ b/solution.py
@@ -268,15 +268,6 @@
 ):
     me_s = lax.axis_index("space")
     me_b = lax.axis_index("batch")
-    def fetch(src, dst, index):
-        copy = pltpu.make_async_copy(src, dst, in_sem.at[index])
-        copy.start()
-        return copy
-
-    x_copies = [fetch(x_hbm.at[0], x_ref.at[0], 0)]
-    three_copy = fetch(three_hbm, three_ref, 2)
-    one_copy = fetch(one_hbm, one_ref, 3)
-    x_copies.append(fetch(x_hbm.at[1], x_ref.at[1], 1))
     barrier = pltpu.get_barrier_semaphore()
 
     def each_space_peer(body):
@@ -304,6 +295,15 @@
 
     each_batch_peer(greet_batch)
 
+    def fetch(src, dst, index):
+        copy = pltpu.make_async_copy(src, dst, in_sem.at[index])
+        copy.start()
+        return copy
+
+    x_copies = [fetch(x_hbm.at[0], x_ref.at[0], 0)]
+    three_copy = fetch(three_hbm, three_ref, 2)
+    one_copy = fetch(one_hbm, one_ref, 3)
+    x_copies.append(fetch(x_hbm.at[1], x_ref.at[1], 1))
     small_copies = [
         fetch(src, dst, 4 + index)
         for index, (src, dst) in enumerate(
@@ -520,6 +520,9 @@
                 pl.ds(owner * SLOTS + slot, K3, stride=K2), :
             ].astype(BF16)
 
+    def returned(dst, phase, index, owner):
+        dst[phase, index] = bz[pl.ds(pl.multiple_of(owner * 32, 32), 32), :].astype(BF16)
+
     def slots_in(phase):
         bz[...] = brecv[phase].reshape(NB * 32, 128).astype(F32)
         for slot in range(L2):
@@ -542,8 +545,7 @@
         lefts_v[index] = left
         both = dot(left[:, :C], w_v[slot, k])
         bz[pl.ds(index, NB, stride=32), :] = both[:8] + sign * pltpu.roll(both[8:], 64, 1)
-    bsend[1] = bz[...].astype(BF16).reshape(NB, 32, 128)
-    batch_start(1)
+    batch_start(1, returned)
     batch_wait(1)
     slots_in(1)
     out_spec = []
@@ -699,8 +701,7 @@
         weights = w_v[slot, k]
         both = dot_nt(grads, jnp.concatenate([weights, weights], axis=0))
         bz[pl.ds(index, NB, stride=32), :] = jnp.where(sign < 0.0, both[:8], both[8:])
-    bsend[3] = bz[...].astype(BF16).reshape(NB, 32, 128)
-    batch_start(3)
+    batch_start(3, returned)
 
     drain(r_batch.at[pl.ds(0, NB - 1)], rrecv.at[0])
     part_near[...] = jnp.sum(r_batch[...], axis=0)
@@ -712,10 +713,6 @@
         send(part_near, r_near.at[near], 1, {"space": peer})
 
     r_near[near] = part_near[...]
-
-    mix_channels(gp_v, kron_back_v, False)
-    skip_copy = pltpu.make_async_copy(skip_v, skip_out_hbm, out_sem.at[2])
-    skip_copy.start()
 
     batch_wait(3)
     slots_in(3)
@@ -744,6 +741,10 @@
         dg_v[slot, k] = dot_tn(lefts_v[index], grads_v[index])[:C]
     dg_copy = pltpu.make_async_copy(dg_v, dg_hbm.at[0], out_sem.at[1])
     dg_copy.start()
+
+    mix_channels(gp_v, kron_back_v, False)
+    skip_copy = pltpu.make_async_copy(skip_v, skip_out_hbm, out_sem.at[2])
+    skip_copy.start()
 
     drain(r_far.at[pl.ds(0, 3)], rrecv.at[2])
     part_all[...] = jnp.sum(r_far[...], axis=0)

time: 77.2 us -> 77.2 us (level)
  no operation moved by 1% of the time
where the time goes in v4:
time: 77.2 us; the launch traced here: 76.1 us
  Pallas kernels  75.3 us (98%)
  between operations  0.82 us (1%)
    pallas_call x1, Pallas kernels, local(): pl.pallas_call(kernel, out_shape=(jax.ShapeDtypeStruct(field, BF16), jax....  70.6 us
    pallas_call x1, Pallas kernels, local(): pl.pallas_call(finish_kernel, out_shape=tuple((jax.ShapeDtypeStruct(*resu...  4.69 us

profile of v4, /device:TPU:1, one launch (start us, length us, event | category | flops | bytes accessed | tf_op | source)
XLA Modules:
  0.0 76.1 jit_solution(1606697341423416431)
XLA Ops:
  0.6 70.6 %shard_map.276 = (bf16[2,8,8,64,128]{4,3,2,1,0:T(8,128)(2,1)}, bf16[2,8,8,64,128]{4,3,2,1,0:T(8,128)(2,1)}, bf16[8,8,64,128]{3,2,1,0:T(8,128)(2,1)}, f32[1,2,16,...) custom-call(s32[16]{0:T(128)} %owner_ref.1, f32[64]{0:T(128)} %bias_ref.1, ...), custom_call_target="tpu_custom_call" | custom-call | tf_op jit(solution)/shard_map/pallas_call | solution.py:939
  71.2 4.7 %shard_map.277 = (bf16[2,8,8,64,128]{4,3,2,1,0:T(8,128)(2,1)}, bf16[2,8,8,64,128]{4,3,2,1,0:T(8,128)(2,1)}, f32[1,2,16,64,128]{4,3,2,1,0:T(8,128)}, f32[16,64]{1...) custom-call(bf16[32,16,128]{2,1,0:T(8,128)(2,1)} %get-tuple-element., ...), custom_call_target="tpu_custom_call" | custom-call | tf_op jit(solution)/shard_map/pallas_call | solution.py:1013
